TPU v7x, 768 devices: a whole 4x8x12 slice. The times are simulated.
768 devices in a mesh: row: 8 (over z_lo, core), col: 96 (over y, z_hi, x).
Axes of the slice: x: 4, y: 8, z: 12 (z_hi: 3, z_lo: 4; z = z_hi * 4 + z_lo), core: 2. Of those that a mesh axis runs over, the one named last changes fastest.
Arguments:
- block_values: bfloat16 [1024, 393216], P('row', 'col'), may hold values from -6 to 6
- slot_rows: int32 [8, 12288], P('row', 'col'), may hold values from 0 to 383
- slot_cols: int32 [8, 12288], P('row', 'col'), may hold values from 0 to 31
- tile_counts: int32 [8, 96], P('row', 'col'), may hold values from 32 to 128, as said below
- prolong_blocks: bfloat16 [3072, 1024], P(('row', 'col')), may hold values from -0.75 to 0.75
- aggregate_ids: int32 [3072], P(('row', 'col')), may hold values from 0 to 1, as said below
Outputs:
- coarse_matrix: bfloat16 [24576, 24576], P('row', 'col')
Inputs may be any that keep to these rules, and one draw needn't show every extreme that they name: `slot_rows`: slots of one tile may name the same block pair; their products add. `tile_counts`: slots at and beyond a tile's count are ignored; some tile is full. `aggregate_ids`: the 4 blocks of one device name each of its 2 aggregates at least once.
All inputs are finite; a program needn't handle non-finite values.
Results may differ from a plain program's by a relative error of at most 0.001.
Values may be sent and summed in bfloat16 or wider, within the bound.
No kernel may reach another device: no remote copies, remote signals or barrier semaphores. Data moves between devices by JAX's collectives and lax.ppermute only.
A program may use at most 64 MiB of HBM per device.

v0:
```python
import jax
import jax.numpy as jnp
from jax import lax
from jax.experimental import pallas as pl
from jax.experimental.pallas import tpu as pltpu
from jax.sharding import PartitionSpec as P

BS = 64
CB = 16
AD = 2
QD = 4
NEAR = 4
LANES = 128
PARTS = 2
CHUNKS = 6
WIDE = BS * CB + LANES


def hot_slots(index, blocks):
    slots = index.shape[1]
    hot = lax.broadcasted_iota(jnp.int32, (blocks, slots), 0) == index
    return hot.astype(jnp.float32).T.astype(jnp.bfloat16)


def slots_to_lanes(picked, target):
    for k in range(WIDE // LANES):
        target[pl.ds(k * LANES, LANES), :] = picked[:, k * LANES:(k + 1) * LANES].T


def right_kernel(me_ref, a_ref, held_ref, rest_ref, row_ref, col_ref, z_ref, coarse_ref, pick_ref, at, rt):
    f32 = jnp.float32
    slots = a_ref.shape[0]
    slot_col = col_ref[...]
    half = held_ref.shape[0]
    place = ((slot_col >> 2) ^ me_ref[0, 0]) * QD + (slot_col & (QD - 1))
    picked = jnp.dot(hot_slots(place, half), held_ref[...], preferred_element_type=f32)
    picked += jnp.dot(hot_slots(place - half, half), rest_ref[...], preferred_element_type=f32)
    slots_to_lanes(picked, rt)
    for k in range(BS * BS // LANES):
        at[pl.ds(k * LANES, LANES), :] = a_ref[:, k * LANES:(k + 1) * LANES].astype(f32).T

    group = 8

    def x_block(b, carry):
        base = pl.multiple_of(b * (group * BS), group * BS)
        sums = [jnp.zeros((CB, slots), f32) for _ in range(group)]
        for z in range(BS):
            r = rt[pl.ds(z * CB, CB), :]
            for xi in range(group):
                sums[xi] = sums[xi] + at[pl.ds(base + (xi * BS + z), 1), :] * r
        for xi in range(group):
            z_ref[pl.ds(pl.multiple_of(b * (group * CB), group * CB) + xi * CB, CB), :] = sums[xi]
        return carry

    lax.fori_loop(0, BS // group, x_block, 0)
    coarse_ref[...] = (slot_col >> 2) * AD + rt[pl.ds(BS * CB, 1), :].astype(jnp.int32)
    slot_row = row_ref[...]
    device = slot_row >> 2
    blocks = pick_ref.shape[1]
    place = (device & (NEAR - 1)) * (blocks // NEAR) + (device >> 2) * QD + (slot_row & (QD - 1))
    pick_ref[...] = hot_slots(place, blocks)


def left_kernel(count_ref, left_ref, pick_ref, z_ref, coarse_ref, row_ref, out_ref, lt, acc0, acc1, staged, sems):
    f32 = jnp.float32
    bf16 = jnp.bfloat16
    slots = z_ref.shape[1]
    slots_to_lanes(jnp.dot(pick_ref[...], left_ref[...], preferred_element_type=f32), lt)

    def x_step(b, sums):
        base = pl.multiple_of(b * (8 * CB), 8 * CB)
        sums = list(sums)
        for xi in range(8):
            zx = z_ref[pl.ds(base + xi * CB, CB), :]
            for u in range(CB):
                sums[u] = sums[u] + lt[pl.ds(base + (xi * CB + u), 1), :] * zx
        return tuple(sums)

    terms = lax.fori_loop(0, BS // 8, x_step, tuple(jnp.zeros((CB, slots), f32) for _ in range(CB)))

    coarse_row = (row_ref[...] >> 2) * AD + lt[pl.ds(BS * CB, 1), :].astype(jnp.int32)
    live = lax.broadcasted_iota(jnp.int32, (1, slots), 1) < count_ref[0, 0]
    coarse_row = jnp.where(live, coarse_row, -1)
    coarse_col = coarse_ref[...]
    rows = out_ref.shape[0] // CB
    cols = out_ref.shape[1] // CB
    hot = (lax.broadcasted_iota(jnp.int32, (rows, slots), 0) == coarse_row).astype(bf16)
    hot = jnp.concatenate([hot] * PARTS, axis=1)
    masks = [jnp.broadcast_to((coarse_col == v).astype(f32), (CB, slots)).astype(bf16) for v in range(cols)]

    for u in range(CB):
        rest = terms[u]
        placed = []
        for _ in range(PARTS):
            part = rest.astype(bf16)
            rest = rest - part.astype(f32)
            placed.append(jnp.concatenate([mask * part for mask in masks], axis=0))
        placed = jnp.concatenate(placed, axis=1)
        summed = lax.dot_general(hot, placed, (((1,), (1,)), ((), ())), preferred_element_type=f32)
        acc0[pl.ds(u, rows, stride=CB), :] = summed[:, :LANES]
        acc1[pl.ds(u, rows, stride=CB), :] = summed[:, LANES:]

    copies = []
    chunk = out_ref.shape[0] // CHUNKS
    for k in range(CHUNKS):
        part = pl.ds(k * chunk, chunk)
        staged[part, :LANES] = acc0[part, :].astype(bf16)
        staged[part, LANES:] = acc1[part, :].astype(bf16)
        copies.append(pltpu.make_async_copy(staged.at[part, :], out_ref.at[part, :], sems.at[k]))
        copies[-1].start()
    for copy in copies:
        copy.wait()


def right_products(me, values, held, rest, slot_row, slot_col, blocks):
    slots = values.shape[0]
    f32 = jnp.float32
    vmem = pl.BlockSpec(memory_space=pltpu.VMEM)
    return pl.pallas_call(
        right_kernel,
        out_shape=[
            jax.ShapeDtypeStruct((BS * CB, slots), f32),
            jax.ShapeDtypeStruct((1, slots), jnp.int32),
            jax.ShapeDtypeStruct((slots, blocks), jnp.bfloat16),
        ],
        in_specs=[pl.BlockSpec(memory_space=pltpu.SMEM)] + [vmem] * 5,
        out_specs=[vmem] * 3,
        scratch_shapes=[pltpu.VMEM((BS * BS, slots), f32), pltpu.VMEM((WIDE, slots), f32)],
        compiler_params=pltpu.CompilerParams(vmem_limit_bytes=24 * 1024 * 1024),
    )(me, values, held, rest, slot_row, slot_col)


def coarse_tile(live_count, left, pick, z, coarse_col, slot_row, rows, cols):
    slots = z.shape[1]
    f32 = jnp.float32
    vmem = pl.BlockSpec(memory_space=pltpu.VMEM)
    return pl.pallas_call(
        left_kernel,
        out_shape=jax.ShapeDtypeStruct((rows, cols), jnp.bfloat16),
        in_specs=[pl.BlockSpec(memory_space=pltpu.SMEM)] + [vmem] * 5,
        out_specs=pl.BlockSpec(memory_space=pl.ANY),
        scratch_shapes=[
            pltpu.VMEM((WIDE, slots), f32),
            pltpu.VMEM((rows, LANES), f32),
            pltpu.VMEM((rows, LANES), f32),
            pltpu.VMEM((rows, cols), jnp.bfloat16),
            pltpu.SemaphoreType.DMA((CHUNKS,)),
        ],
        compiler_params=pltpu.CompilerParams(vmem_limit_bytes=24 * 1024 * 1024),
    )(live_count, left, pick, z, coarse_col, slot_row)


def payload_kernel(ids_ref, blocks_ref, mine_ref, copies_ref):
    row = lax.broadcasted_iota(jnp.int32, (QD, LANES), 0)
    ids = jnp.zeros((QD, LANES), jnp.float32)
    for t in range(QD):
        ids = jnp.where(row == t, ids_ref[t].astype(jnp.float32), ids)
    whole = jnp.concatenate([blocks_ref[...].astype(jnp.float32), ids], axis=1).astype(jnp.bfloat16)
    mine_ref[0] = whole
    for k in range(copies_ref.shape[0]):
        copies_ref[k] = whole


def payload(blocks, ids, count):
    vmem = pl.BlockSpec(memory_space=pltpu.VMEM)
    return pl.pallas_call(
        payload_kernel,
        out_shape=[
            pltpu.VMEM((1, QD, WIDE), jnp.bfloat16),
            jax.ShapeDtypeStruct((count, QD, WIDE), jnp.bfloat16),
        ],
        in_specs=[pl.BlockSpec(memory_space=pltpu.SMEM), vmem],
        out_specs=[vmem, vmem],
    )(ids, blocks)


def everywhere(block, axis, size, groups=None):
    copies = jnp.broadcast_to(block[None], (size,) + block.shape)
    return lax.all_to_all(copies, axis, 0, 0, axis_index_groups=groups, tiled=True)


def shards(block_values, slot_rows, slot_cols, tile_counts, prolong_blocks, aggregate_ids):
    row_size = lax.axis_size("row")
    col_size = lax.axis_size("col")
    planes = col_size // NEAR
    mine, copies = payload(prolong_blocks, aggregate_ids, planes)
    held = mine
    step = 1
    while 2 * step < row_size:
        held = jnp.concatenate([held, lax.ppermute(held, "row", [(r ^ step, r) for r in range(row_size)])], axis=0)
        step *= 2
    rest = lax.ppermute(held, "row", [(r ^ step, r) for r in range(row_size)])
    held = held.reshape(step * QD, WIDE)
    rest = rest.reshape(step * QD, WIDE)
    me = lax.axis_index("row").astype(jnp.int32).reshape(1, 1)
    yz_groups = [[p * NEAR + x for p in range(planes)] for x in range(NEAR)]
    x_groups = [[p * NEAR + x for x in range(NEAR)] for p in range(planes)]
    plane = lax.all_to_all(copies, "col", 0, 0, axis_index_groups=yz_groups, tiled=True).reshape(planes * QD, WIDE)
    plane, held = lax.optimization_barrier((plane, held))
    left = everywhere(plane, "col", NEAR, x_groups).reshape(col_size * QD, WIDE)
    z, coarse_col, pick = right_products(me, block_values, held, rest, slot_rows, slot_cols, col_size * QD)
    return coarse_tile(
        tile_counts, left, pick, z, coarse_col, slot_rows, col_size * AD * CB, row_size * AD * CB
    )


def solution(mesh):
    placed = (
        P("row", "col"),
        P("row", "col"),
        P("row", "col"),
        P("row", "col"),
        P(("row", "col"), None),
        P(("row", "col")),
    )
    return jax.shard_map(
        shards, mesh=mesh, in_specs=placed, out_specs=P("row", "col"), check_vma=False
    )
```

profile of v0, /device:TPU:192, one launch (start us, length us, event | category | flops | bytes accessed | tf_op | source)
XLA Modules:
  0.0 57.4 jit_solution(13147608365944178351)
XLA Ops:
  0.0 1.4 %shard_map.64 = (bf16[1,4,1152]{2,1,0:T(4,128)(2,1)S(1)}, bf16[24,4,1152]{2,1,0:T(4,128)(2,1)}) custom-call(s32[4]{0:T(128)} %ids_ref.1, bf16[4,1024]{1,0:T(4,128)(2,1)} %blocks_ref.1), custom_call_target="tpu_custom_call" | custom-call | tf_op jit(solution)/shard_map/pallas_call | solution.py:166
  1.4 16.7 %all-to-all-start = ((bf16[24,4,1152]{2,1,0:T(4,128)(2,1)}), bf16[24,4,1152]{2,1,0:T(4,128)(2,1)S(1)}, u32[]{:S(2)}, u32[]{:S(2)}) async-start(bf16[24,4,1152]{2,1,0:T(4,128)(2,1)} %get-tuple-element.12), calls=%async_computation | async-start | bytes 442368 | tf_op jit(solution)/shard_map/all_to_all | solution.py:198
  18.2 1.9 %collective-permute-start = (bf16[1,4,1152]{2,1,0:T(4,128)(2,1)S(1)}, bf16[1,4,1152]{2,1,0:T(4,128)(2,1)S(1)}, u32[]{:S(2)}, u32[]{:S(2)}) collective-permute-start(bf16[1,4,1152]{2,1,0:T(4,128)(2,1)S(1)} %get-tuple-element.13), channel_id=1, source_target_pairs={{96,0},{0,96},{288,192},{192,288},{480,384},{384,480},{672,576},{5... | collective-permute-start | bytes 27656 | tf_op jit(solution)/shard_map/ppermute | solution.py:190
  20.1 1.1 %collective-permute-done = bf16[1,4,1152]{2,1,0:T(4,128)(2,1)S(1)} collective-permute-done((bf16[1,4,1152]{2,1,0:T(4,128)(2,1)S(1)}, bf16[1,4,1152]{2,1,0:T(4,128)(2,1)S(1)}, u32[]{:S(2)}, u32[]{:S(2)}) %collective-permute-start) | collective-permute-done | bytes 9248 | tf_op jit(solution)/shard_map/ppermute | solution.py:190
  21.3 2.5 %collective-permute-start.1 = (bf16[2,4,1152]{2,1,0:T(4,128)(2,1)S(1)}, bf16[2,4,1152]{2,1,0:T(4,128)(2,1)S(1)}, u32[]{:S(2)}, u32[]{:S(2)}) collective-permute-start(bf16[2,4,1152]{2,1,0:T(4,128)(2,1)S(1)} %pad_maximum_fusion), channel_id=1, source_target_pairs={{192,0},{288,96},{0,192},{96,288},{576,384},{672,480},{384,576},{4... | collective-permute-start | bytes 55304 | tf_op jit(solution)/shard_map/ppermute | solution.py:190
  23.7 3.2 %collective-permute-done.1 = bf16[2,4,1152]{2,1,0:T(4,128)(2,1)S(1)} collective-permute-done((bf16[2,4,1152]{2,1,0:T(4,128)(2,1)S(1)}, bf16[2,4,1152]{2,1,0:T(4,128)(2,1)S(1)}, u32[]{:S(2)}, u32[]{:S(2)}) %collective-permute-start.1) | collective-permute-done | bytes 18464 | tf_op jit(solution)/shard_map/ppermute | solution.py:190
  26.9 8.4 %all-to-all-done = bf16[24,4,1152]{2,1,0:T(4,128)(2,1)S(1)} async-done(((bf16[24,4,1152]{2,1,0:T(4,128)(2,1)}), bf16[24,4,1152]{2,1,0:T(4,128)(2,1)S(1)}, u32[]{:S(2)}, u32[]{:S(2)}) %all-to-all-start) | async-done | bytes 221216 | tf_op jit(solution)/shard_map/all_to_all | solution.py:198
  35.4 0.1 reshape.16
  35.4 0.0 copy-start
  35.4 0.0 copy-start.1
  35.5 0.0 copy-start.2
  35.5 1.0 %broadcast_in_dim.2 = bf16[4,96,1152]{2,1,0:T(8,128)(2,1)} broadcast(bf16[96,1152]{1,0:T(8,128)(2,1)S(1)} %reshape.16), dimensions={1,2} | broadcast | bytes 1105920 | tf_op jit(solution)/shard_map/broadcast_in_dim | solution.py:178
  36.4 4.3 %all-to-all-start.1 = ((bf16[4,96,1152]{2,1,0:T(8,128)(2,1)}), bf16[4,96,1152]{2,1,0:T(8,128)(2,1)S(1)}, u32[]{:S(2)}, u32[]{:S(2)}) async-start(bf16[4,96,1152]{2,1,0:T(8,128)(2,1)} %broadcast_in_dim.2), calls=%async_computation.1 | async-start | bytes 1769472 | tf_op jit(solution)/shard_map/all_to_all | solution.py:179
  40.7 1.9 %collective-permute-start.2 = (bf16[4,4,1152]{2,1,0:T(4,128)(2,1)S(1)}, bf16[4,4,1152]{2,1,0:T(4,128)(2,1)S(1)}, u32[]{:S(2)}, u32[]{:S(2)}) collective-permute-start(bf16[4,4,1152]{2,1,0:T(4,128)(2,1)S(1)} %constant_dynamic-update-slice_fusion), channel_id=1, source_target_pairs={{384,0},{480,96},{576,192},{672,288},{0,384},{96,480},{192,576},{2... | collective-permute-start | bytes 110600 | tf_op jit(solution)/shard_map/ppermute | solution.py:192
  43.3 4.2 %collective-permute-done.2 = bf16[4,4,1152]{2,1,0:T(4,128)(2,1)S(1)} collective-permute-done((bf16[4,4,1152]{2,1,0:T(4,128)(2,1)S(1)}, bf16[4,4,1152]{2,1,0:T(4,128)(2,1)S(1)}, u32[]{:S(2)}, u32[]{:S(2)}) %collective-permute-start.2) | collective-permute-done | bytes 36896 | tf_op jit(solution)/shard_map/ppermute | solution.py:192
  47.5 0.0 copy-done
  47.5 0.0 copy-done.1
  47.5 0.0 copy-done.2
  47.5 3.6 %shard_map.65 = (f32[1024,128]{1,0:T(8,128)S(1)}, s32[1,128]{1,0:T(1,128)S(1)}, bf16[128,384]{1,0:T(8,128)(2,1)S(1)}) custom-call(s32[1,1]{1,0:T(1,128)} %bitcast.1.me_ref, bf16[128,4096]{1,0:T(8,128)(2,1)S(1)} %copy-done, bf16[16,1152]{1,0:T(8,128)(2,1)S(1)} %reshape.17.held_ref, bf16[16,1152]{1,0:T(8,128)(2,1)S(1)} %reshape.20.rest_ref, ...), custom_call_target="tpu_custom_call" | custom-call | tf_op jit(solution)/shard_map/pallas_call | solution.py:119
  51.1 2.7 %all-to-all-done.1 = bf16[4,96,1152]{2,1,0:T(8,128)(2,1)S(1)} async-done(((bf16[4,96,1152]{2,1,0:T(8,128)(2,1)}), bf16[4,96,1152]{2,1,0:T(8,128)(2,1)S(1)}, u32[]{:S(2)}, u32[]{:S(2)}) %all-to-all-start.1) | async-done | bytes 884768 | tf_op jit(solution)/shard_map/all_to_all | solution.py:179
  53.8 3.6 %shard_map.66 = bf16[3072,256]{1,0:T(8,128)(2,1)} custom-call(s32[1,1]{1,0:T(1,128)S(6)} %copy.9.count_ref, bf16[384,1152]{1,0:T(8,128)(2,1)S(1)} %bitcast.2, bf16[128,384]{1,0:T(8,128)(2,1)S(1)} %get-tuple-element.16.pick_ref, f32[1024,128]{1,0:T(8,128)S(1)} %get-tuple-element.17.z_ref, s32[1,128]{1,0:T(1,128)S(1)} %get-tuple-element.18.coarse_ref, ...), custom_call_target="tpu_custom_call" | custom-call | tf_op jit(solution)/shard_map/pallas_call | solution.py:137
  (6 shorter events, 0.1 us)
Async XLA Ops:
  1.4 33.9 %all-to-all-start = ((bf16[24,4,1152]{2,1,0:T(4,128)(2,1)}), bf16[24,4,1152]{2,1,0:T(4,128)(2,1)S(1)}, u32[]{:S(2)}, u32[]{:S(2)}) async-start(bf16[24,4,1152]{2,1,0:T(4,128)(2,1)} %get-tuple-element.12), calls=%async_computation | async-start | bytes 442368 | tf_op jit(solution)/shard_map/all_to_all | solution.py:198
  18.2 3.1 %collective-permute-start = (bf16[1,4,1152]{2,1,0:T(4,128)(2,1)S(1)}, bf16[1,4,1152]{2,1,0:T(4,128)(2,1)S(1)}, u32[]{:S(2)}, u32[]{:S(2)}) collective-permute-start(bf16[1,4,1152]{2,1,0:T(4,128)(2,1)S(1)} %get-tuple-element.13), channel_id=1, source_target_pairs={{96,0},{0,96},{288,192},{192,288},{480,384},{384,480},{672,576},{5... | collective-permute-start | bytes 27656 | tf_op jit(solution)/shard_map/ppermute | solution.py:190
  21.3 5.7 %collective-permute-start.1 = (bf16[2,4,1152]{2,1,0:T(4,128)(2,1)S(1)}, bf16[2,4,1152]{2,1,0:T(4,128)(2,1)S(1)}, u32[]{:S(2)}, u32[]{:S(2)}) collective-permute-start(bf16[2,4,1152]{2,1,0:T(4,128)(2,1)S(1)} %pad_maximum_fusion), channel_id=1, source_target_pairs={{192,0},{288,96},{0,192},{96,288},{576,384},{672,480},{384,576},{4... | collective-permute-start | bytes 55304 | tf_op jit(solution)/shard_map/ppermute | solution.py:190
  35.4 12.1 %copy-start = (bf16[128,4096]{1,0:T(8,128)(2,1)S(1)}, bf16[128,4096]{1,0:T(8,128)(2,1)}, u32[]{:S(2)}) copy-start(bf16[128,4096]{1,0:T(8,128)(2,1)} %a_ref.1) | copy-start | bytes 3145732
  35.4 12.1 %copy-start.1 = (s32[1,128]{1,0:T(1,128)S(1)}, s32[1,128]{1,0:T(1,128)}, u32[]{:S(2)}) copy-start(s32[1,128]{1,0:T(1,128)} %row_ref.3) | copy-start | bytes 1540
  35.5 12.1 %copy-start.2 = (s32[1,128]{1,0:T(1,128)S(1)}, s32[1,128]{1,0:T(1,128)}, u32[]{:S(2)}) copy-start(s32[1,128]{1,0:T(1,128)} %col_ref.1) | copy-start | bytes 1540
  36.4 17.4 %all-to-all-start.1 = ((bf16[4,96,1152]{2,1,0:T(8,128)(2,1)}), bf16[4,96,1152]{2,1,0:T(8,128)(2,1)S(1)}, u32[]{:S(2)}, u32[]{:S(2)}) async-start(bf16[4,96,1152]{2,1,0:T(8,128)(2,1)} %broadcast_in_dim.2), calls=%async_computation.1 | async-start | bytes 1769472 | tf_op jit(solution)/shard_map/all_to_all | solution.py:179
  40.7 6.7 %collective-permute-start.2 = (bf16[4,4,1152]{2,1,0:T(4,128)(2,1)S(1)}, bf16[4,4,1152]{2,1,0:T(4,128)(2,1)S(1)}, u32[]{:S(2)}, u32[]{:S(2)}) collective-permute-start(bf16[4,4,1152]{2,1,0:T(4,128)(2,1)S(1)} %constant_dynamic-update-slice_fusion), channel_id=1, source_target_pairs={{384,0},{480,96},{576,192},{672,288},{0,384},{96,480},{192,576},{2... | collective-permute-start | bytes 110600 | tf_op jit(solution)/shard_map/ppermute | solution.py:192
where the time goes:
time: 57.8 us; the launch traced here: 57.4 us
  starting transfers between devices  27.3 us (47%)
  waiting for transfers between devices  19.6 us (34%)
  Pallas kernels  8.64 us (15%)
  local copies, waits for them, and re-layouts  1.12 us (2%)
  between operations  0.77 us (1%)
    all_to_all x1, starting transfers between devices, shards(): lax.all_to_all(copies, 'col', 0, 0, axis_index_groups=yz_groups, tiled=True)  16.7 us
    all_to_all x1, waiting for transfers between devices, shards(): lax.all_to_all(copies, 'col', 0, 0, axis_index_groups=yz_groups, tiled=True)  8.42 us
    ppermute x2, starting transfers between devices, shards(): lax.ppermute(held, 'row', [(r ^ step, r) for r in range(row_size)])  4.38 us
    ppermute x2, waiting for transfers between devices, shards(): lax.ppermute(held, 'row', [(r ^ step, r) for r in range(row_size)])  4.29 us
    all_to_all x1, starting transfers between devices, everywhere(): lax.all_to_all(copies, axis, 0, 0, axis_index_groups=groups, tiled=True)  4.29 us
    ppermute x1, waiting for transfers between devices, shards(): rest = lax.ppermute(held, 'row', [(r ^ step, r) for r in range(row_size)])  4.17 us
    pallas_call x1, Pallas kernels, coarse_tile(): pl.pallas_call(left_kernel, out_shape=jax.ShapeDtypeStruct((rows, cols),...  3.64 us
    pallas_call x1, Pallas kernels, right_products(): pl.pallas_call(right_kernel, out_shape=[jax.ShapeDtypeStruct((BS * CB, sl...  3.57 us
  transfers between devices with their start and end apart: 5, of which 5 were waited for; matrix products, arithmetic and copies ran while one was open for 0% of the time, Pallas kernels for 6%

commit v1 on v0

--- a/solution.py
+++ b/solution.py
@@ -32,7 +32,9 @@
     slots = a_ref.shape[0]
     slot_col = col_ref[...]
     half = held_ref.shape[0]
-    place = ((slot_col >> 2) ^ me_ref[0, 0]) * QD + (slot_col & (QD - 1))
+    away = (slot_col >> 2) ^ me_ref[0, 0]
+    turned = ((away & 1) << 2) | (away & 2) | (away >> 2)
+    place = turned * QD + (slot_col & (QD - 1))
     picked = jnp.dot(hot_slots(place, half), held_ref[...], preferred_element_type=f32)
     picked += jnp.dot(hot_slots(place - half, half), rest_ref[...], preferred_element_type=f32)
     slots_to_lanes(picked, rt)
@@ -185,13 +187,13 @@
     planes = col_size // NEAR
     mine, copies = payload(prolong_blocks, aggregate_ids, planes)
     held = mine
-    step = 1
-    while 2 * step < row_size:
+    step = row_size // 2
+    while step > 1:
         held = jnp.concatenate([held, lax.ppermute(held, "row", [(r ^ step, r) for r in range(row_size)])], axis=0)
-        step *= 2
+        step //= 2
     rest = lax.ppermute(held, "row", [(r ^ step, r) for r in range(row_size)])
-    held = held.reshape(step * QD, WIDE)
-    rest = rest.reshape(step * QD, WIDE)
+    held = held.reshape(row_size // 2 * QD, WIDE)
+    rest = rest.reshape(row_size // 2 * QD, WIDE)
     me = lax.axis_index("row").astype(jnp.int32).reshape(1, 1)
     yz_groups = [[p * NEAR + x for p in range(planes)] for x in range(NEAR)]
     x_groups = [[p * NEAR + x for x in range(NEAR)] for p in range(planes)]

time: 57.8 us -> 57.9 us (level)
    all_to_all x1, waiting for transfers between devices: 8.42 us -> 4.67 us  [shards(): lax.all_to_all(copies, 'col', 0, 0, axis_index_groups=yz_groups, tiled=True)]
    ppermute x1, waiting for transfers between devices: 4.17 us -> 0.53 us  [shards(): rest = lax.ppermute(held, 'row', [(r ^ step, r) for r in range(row_size)])]
    all_to_all x1, waiting for transfers between devices: 2.7 us -> 6.34 us  [everywhere(): lax.all_to_all(copies, axis, 0, 0, axis_index_groups=groups, tiled=True)]
    ppermute x2, waiting for transfers between devices: 4.29 us -> 7.74 us  [shards(): lax.ppermute(held, 'row', [(r ^ step, r) for r in range(row_size)])]
where the time goes in v1:
time: 57.9 us; the launch traced here: 57.6 us
  starting transfers between devices  27.7 us (48%)
  waiting for transfers between devices  19.3 us (33%)
  Pallas kernels  8.64 us (15%)
  local copies, waits for them, and re-layouts  1.12 us (2%)
  between operations  0.77 us (1%)
    all_to_all x1, starting transfers between devices, shards(): lax.all_to_all(copies, 'col', 0, 0, axis_index_groups=yz_groups, tiled=True)  16.7 us
    ppermute x2, waiting for transfers between devices, shards(): lax.ppermute(held, 'row', [(r ^ step, r) for r in range(row_size)])  7.74 us
    all_to_all x1, waiting for transfers between devices, everywhere(): lax.all_to_all(copies, axis, 0, 0, axis_index_groups=groups, tiled=True)  6.34 us
    ppermute x2, starting transfers between devices, shards(): lax.ppermute(held, 'row', [(r ^ step, r) for r in range(row_size)])  4.81 us
    all_to_all x1, waiting for transfers between devices, shards(): lax.all_to_all(copies, 'col', 0, 0, axis_index_groups=yz_groups, tiled=True)  4.67 us
    all_to_all x1, starting transfers between devices, everywhere(): lax.all_to_all(copies, axis, 0, 0, axis_index_groups=groups, tiled=True)  4.29 us
    pallas_call x1, Pallas kernels, coarse_tile(): pl.pallas_call(left_kernel, out_shape=jax.ShapeDtypeStruct((rows, cols),...  3.65 us
    pallas_call x1, Pallas kernels, right_products(): pl.pallas_call(right_kernel, out_shape=[jax.ShapeDtypeStruct((BS * CB, sl...  3.57 us
  transfers between devices with their start and end apart: 5, of which 5 were waited for; matrix products, arithmetic and copies ran while one was open for 0% of the time, Pallas kernels for 6%

profile of v1, /device:TPU:192, one launch (start us, length us, event | category | flops | bytes accessed | tf_op | source)
XLA Modules:
  0.0 57.6 jit_solution(11234930627473038907)
XLA Ops:
  0.0 1.4 %shard_map.64 = (bf16[1,4,1152]{2,1,0:T(4,128)(2,1)S(1)}, bf16[24,4,1152]{2,1,0:T(4,128)(2,1)}) custom-call(s32[4]{0:T(128)} %ids_ref.1, bf16[4,1024]{1,0:T(4,128)(2,1)} %blocks_ref.1), custom_call_target="tpu_custom_call" | custom-call | tf_op jit(solution)/shard_map/pallas_call | solution.py:168
  1.4 16.7 %all-to-all-start = ((bf16[24,4,1152]{2,1,0:T(4,128)(2,1)}), bf16[24,4,1152]{2,1,0:T(4,128)(2,1)S(1)}, u32[]{:S(2)}, u32[]{:S(2)}) async-start(bf16[24,4,1152]{2,1,0:T(4,128)(2,1)} %get-tuple-element.12), calls=%async_computation | async-start | bytes 442368 | tf_op jit(solution)/shard_map/all_to_all | solution.py:200
  18.2 2.5 %collective-permute-start = (bf16[1,4,1152]{2,1,0:T(4,128)(2,1)S(1)}, bf16[1,4,1152]{2,1,0:T(4,128)(2,1)S(1)}, u32[]{:S(2)}, u32[]{:S(2)}) collective-permute-start(bf16[1,4,1152]{2,1,0:T(4,128)(2,1)S(1)} %get-tuple-element.13), channel_id=1, source_target_pairs={{384,0},{480,96},{576,192},{672,288},{0,384},{96,480},{192,576},{2... | collective-permute-start | bytes 27656 | tf_op jit(solution)/shard_map/ppermute | solution.py:192
  20.6 4.1 %collective-permute-done = bf16[1,4,1152]{2,1,0:T(4,128)(2,1)S(1)} collective-permute-done((bf16[1,4,1152]{2,1,0:T(4,128)(2,1)S(1)}, bf16[1,4,1152]{2,1,0:T(4,128)(2,1)S(1)}, u32[]{:S(2)}, u32[]{:S(2)}) %collective-permute-start) | collective-permute-done | bytes 9248 | tf_op jit(solution)/shard_map/ppermute | solution.py:192
  24.8 2.4 %collective-permute-start.1 = (bf16[2,4,1152]{2,1,0:T(4,128)(2,1)S(1)}, bf16[2,4,1152]{2,1,0:T(4,128)(2,1)S(1)}, u32[]{:S(2)}, u32[]{:S(2)}) collective-permute-start(bf16[2,4,1152]{2,1,0:T(4,128)(2,1)S(1)} %pad_maximum_fusion), channel_id=1, source_target_pairs={{192,0},{288,96},{0,192},{96,288},{576,384},{672,480},{384,576},{4... | collective-permute-start | bytes 55304 | tf_op jit(solution)/shard_map/ppermute | solution.py:192
  27.2 3.6 %collective-permute-done.1 = bf16[2,4,1152]{2,1,0:T(4,128)(2,1)S(1)} collective-permute-done((bf16[2,4,1152]{2,1,0:T(4,128)(2,1)S(1)}, bf16[2,4,1152]{2,1,0:T(4,128)(2,1)S(1)}, u32[]{:S(2)}, u32[]{:S(2)}) %collective-permute-start.1) | collective-permute-done | bytes 18464 | tf_op jit(solution)/shard_map/ppermute | solution.py:192
  30.8 4.7 %all-to-all-done = bf16[24,4,1152]{2,1,0:T(4,128)(2,1)S(1)} async-done(((bf16[24,4,1152]{2,1,0:T(4,128)(2,1)}), bf16[24,4,1152]{2,1,0:T(4,128)(2,1)S(1)}, u32[]{:S(2)}, u32[]{:S(2)}) %all-to-all-start) | async-done | bytes 221216 | tf_op jit(solution)/shard_map/all_to_all | solution.py:200
  35.5 0.1 reshape.16
  35.5 0.0 copy-start
  35.6 0.0 copy-start.1
  35.6 0.0 copy-start.2
  35.6 1.0 %broadcast_in_dim.2 = bf16[4,96,1152]{2,1,0:T(8,128)(2,1)} broadcast(bf16[96,1152]{1,0:T(8,128)(2,1)S(1)} %reshape.16), dimensions={1,2} | broadcast | bytes 1105920 | tf_op jit(solution)/shard_map/broadcast_in_dim | solution.py:180
  36.6 4.3 %all-to-all-start.1 = ((bf16[4,96,1152]{2,1,0:T(8,128)(2,1)}), bf16[4,96,1152]{2,1,0:T(8,128)(2,1)S(1)}, u32[]{:S(2)}, u32[]{:S(2)}) async-start(bf16[4,96,1152]{2,1,0:T(8,128)(2,1)} %broadcast_in_dim.2), calls=%async_computation.1 | async-start | bytes 1769472 | tf_op jit(solution)/shard_map/all_to_all | solution.py:181
  40.9 1.9 %collective-permute-start.2 = (bf16[4,4,1152]{2,1,0:T(4,128)(2,1)S(1)}, bf16[4,4,1152]{2,1,0:T(4,128)(2,1)S(1)}, u32[]{:S(2)}, u32[]{:S(2)}) collective-permute-start(bf16[4,4,1152]{2,1,0:T(4,128)(2,1)S(1)} %constant_dynamic-update-slice_fusion), channel_id=1, source_target_pairs={{96,0},{0,96},{288,192},{192,288},{480,384},{384,480},{672,576},{5... | collective-permute-start | bytes 110600 | tf_op jit(solution)/shard_map/ppermute | solution.py:194
  43.4 0.5 collective-permute-done.2
  44.0 0.0 copy-done
  44.0 0.0 copy-done.1
  44.0 0.0 copy-done.2
  44.0 3.6 %shard_map.65 = (f32[1024,128]{1,0:T(8,128)S(1)}, s32[1,128]{1,0:T(1,128)S(1)}, bf16[128,384]{1,0:T(8,128)(2,1)S(1)}) custom-call(s32[1,1]{1,0:T(1,128)} %bitcast.1.me_ref, bf16[128,4096]{1,0:T(8,128)(2,1)S(1)} %copy-done, bf16[16,1152]{1,0:T(8,128)(2,1)S(1)} %reshape.17.held_ref, bf16[16,1152]{1,0:T(8,128)(2,1)S(1)} %reshape.20.rest_ref, ...), custom_call_target="tpu_custom_call" | custom-call | tf_op jit(solution)/shard_map/pallas_call | solution.py:121
  47.6 6.3 %all-to-all-done.1 = bf16[4,96,1152]{2,1,0:T(8,128)(2,1)S(1)} async-done(((bf16[4,96,1152]{2,1,0:T(8,128)(2,1)}), bf16[4,96,1152]{2,1,0:T(8,128)(2,1)S(1)}, u32[]{:S(2)}, u32[]{:S(2)}) %all-to-all-start.1) | async-done | bytes 884768 | tf_op jit(solution)/shard_map/all_to_all | solution.py:181
  53.9 3.6 %shard_map.66 = bf16[3072,256]{1,0:T(8,128)(2,1)} custom-call(s32[1,1]{1,0:T(1,128)S(6)} %copy.9.count_ref, bf16[384,1152]{1,0:T(8,128)(2,1)S(1)} %bitcast.2, bf16[128,384]{1,0:T(8,128)(2,1)S(1)} %get-tuple-element.16.pick_ref, f32[1024,128]{1,0:T(8,128)S(1)} %get-tuple-element.17.z_ref, s32[1,128]{1,0:T(1,128)S(1)} %get-tuple-element.18.coarse_ref, ...), custom_call_target="tpu_custom_call" | custom-call | tf_op jit(solution)/shard_map/pallas_call | solution.py:139
  (6 shorter events, 0.1 us)
Async XLA Ops:
  1.4 34.1 %all-to-all-start = ((bf16[24,4,1152]{2,1,0:T(4,128)(2,1)}), bf16[24,4,1152]{2,1,0:T(4,128)(2,1)S(1)}, u32[]{:S(2)}, u32[]{:S(2)}) async-start(bf16[24,4,1152]{2,1,0:T(4,128)(2,1)} %get-tuple-element.12), calls=%async_computation | async-start | bytes 442368 | tf_op jit(solution)/shard_map/all_to_all | solution.py:200
  18.2 6.6 %collective-permute-start = (bf16[1,4,1152]{2,1,0:T(4,128)(2,1)S(1)}, bf16[1,4,1152]{2,1,0:T(4,128)(2,1)S(1)}, u32[]{:S(2)}, u32[]{:S(2)}) collective-permute-start(bf16[1,4,1152]{2,1,0:T(4,128)(2,1)S(1)} %get-tuple-element.13), channel_id=1, source_target_pairs={{384,0},{480,96},{576,192},{672,288},{0,384},{96,480},{192,576},{2... | collective-permute-start | bytes 27656 | tf_op jit(solution)/shard_map/ppermute | solution.py:192
  24.8 6.0 %collective-permute-start.1 = (bf16[2,4,1152]{2,1,0:T(4,128)(2,1)S(1)}, bf16[2,4,1152]{2,1,0:T(4,128)(2,1)S(1)}, u32[]{:S(2)}, u32[]{:S(2)}) collective-permute-start(bf16[2,4,1152]{2,1,0:T(4,128)(2,1)S(1)} %pad_maximum_fusion), channel_id=1, source_target_pairs={{192,0},{288,96},{0,192},{96,288},{576,384},{672,480},{384,576},{4... | collective-permute-start | bytes 55304 | tf_op jit(solution)/shard_map/ppermute | solution.py:192
  35.5 8.4 %copy-start = (bf16[128,4096]{1,0:T(8,128)(2,1)S(1)}, bf16[128,4096]{1,0:T(8,128)(2,1)}, u32[]{:S(2)}) copy-start(bf16[128,4096]{1,0:T(8,128)(2,1)} %a_ref.1) | copy-start | bytes 3145732
  35.6 8.4 %copy-start.1 = (s32[1,128]{1,0:T(1,128)S(1)}, s32[1,128]{1,0:T(1,128)}, u32[]{:S(2)}) copy-start(s32[1,128]{1,0:T(1,128)} %row_ref.3) | copy-start | bytes 1540
  35.6 8.4 %copy-start.2 = (s32[1,128]{1,0:T(1,128)S(1)}, s32[1,128]{1,0:T(1,128)}, u32[]{:S(2)}) copy-start(s32[1,128]{1,0:T(1,128)} %col_ref.1) | copy-start | bytes 1540
  36.6 17.4 %all-to-all-start.1 = ((bf16[4,96,1152]{2,1,0:T(8,128)(2,1)}), bf16[4,96,1152]{2,1,0:T(8,128)(2,1)S(1)}, u32[]{:S(2)}, u32[]{:S(2)}) async-start(bf16[4,96,1152]{2,1,0:T(8,128)(2,1)} %broadcast_in_dim.2), calls=%async_computation.1 | async-start | bytes 1769472 | tf_op jit(solution)/shard_map/all_to_all | solution.py:181
  40.9 3.1 %collective-permute-start.2 = (bf16[4,4,1152]{2,1,0:T(4,128)(2,1)S(1)}, bf16[4,4,1152]{2,1,0:T(4,128)(2,1)S(1)}, u32[]{:S(2)}, u32[]{:S(2)}) collective-permute-start(bf16[4,4,1152]{2,1,0:T(4,128)(2,1)S(1)} %constant_dynamic-update-slice_fusion), channel_id=1, source_target_pairs={{96,0},{0,96},{288,192},{192,288},{480,384},{384,480},{672,576},{5... | collective-permute-start | bytes 110600 | tf_op jit(solution)/shard_map/ppermute | solution.py:194

commit v2 on v1

--- a/solution.py
+++ b/solution.py
@@ -186,19 +186,20 @@
     col_size = lax.axis_size("col")
     planes = col_size // NEAR
     mine, copies = payload(prolong_blocks, aggregate_ids, planes)
+    yz_groups = [[p * NEAR + x for p in range(planes)] for x in range(NEAR)]
+    plane = lax.all_to_all(copies, "col", 0, 0, axis_index_groups=yz_groups, tiled=True).reshape(planes * QD, WIDE)
     held = mine
     step = row_size // 2
     while step > 1:
         held = jnp.concatenate([held, lax.ppermute(held, "row", [(r ^ step, r) for r in range(row_size)])], axis=0)
+        if step == row_size // 2:
+            plane, held = lax.optimization_barrier((plane, held))
         step //= 2
     rest = lax.ppermute(held, "row", [(r ^ step, r) for r in range(row_size)])
     held = held.reshape(row_size // 2 * QD, WIDE)
     rest = rest.reshape(row_size // 2 * QD, WIDE)
     me = lax.axis_index("row").astype(jnp.int32).reshape(1, 1)
-    yz_groups = [[p * NEAR + x for p in range(planes)] for x in range(NEAR)]
     x_groups = [[p * NEAR + x for x in range(NEAR)] for p in range(planes)]
-    plane = lax.all_to_all(copies, "col", 0, 0, axis_index_groups=yz_groups, tiled=True).reshape(planes * QD, WIDE)
-    plane, held = lax.optimization_barrier((plane, held))
     left = everywhere(plane, "col", NEAR, x_groups).reshape(col_size * QD, WIDE)
     z, coarse_col, pick = right_products(me, block_values, held, rest, slot_rows, slot_cols, col_size * QD)
     return coarse_tile(

time: 57.9 us -> 59.1 us (1.021)
  the two profiles are of different devices: /device:TPU:192 before, /device:TPU:131 now
where the time goes in v2:
time: 59.1 us; the launch traced here: 58.7 us
  starting transfers between devices  32.2 us (54%)
  waiting for transfers between devices  15.3 us (26%)
  Pallas kernels  9.35 us (16%)
  local copies, waits for them, and re-layouts  1.1 us (2%)
  between operations  0.78 us (1%)
    all_to_all x1, starting transfers between devices, shards(): lax.all_to_all(copies, 'col', 0, 0, axis_index_groups=yz_groups, tiled=True)  17.4 us
    all_to_all x1, waiting for transfers between devices, shards(): lax.all_to_all(copies, 'col', 0, 0, axis_index_groups=yz_groups, tiled=True)  10.4 us
    ppermute x2, starting transfers between devices, shards(): lax.ppermute(held, 'row', [(r ^ step, r) for r in range(row_size)])  6.55 us
    ppermute x2, waiting for transfers between devices, shards(): lax.ppermute(held, 'row', [(r ^ step, r) for r in range(row_size)])  4.77 us
    pallas_call x1, Pallas kernels, right_products(): pl.pallas_call(right_kernel, out_shape=[jax.ShapeDtypeStruct((BS * CB, sl...  4.28 us
    all_to_all x1, starting transfers between devices, everywhere(): lax.all_to_all(copies, axis, 0, 0, axis_index_groups=groups, tiled=True)  4.26 us
    ppermute x1, starting transfers between devices, shards(): rest = lax.ppermute(held, 'row', [(r ^ step, r) for r in range(row_size)])  3.99 us
    pallas_call x1, Pallas kernels, coarse_tile(): pl.pallas_call(left_kernel, out_shape=jax.ShapeDtypeStruct((rows, cols),...  3.65 us
  transfers between devices with their start and end apart: 5, of which 4 were waited for; matrix products, arithmetic and copies ran while one was open for 0% of the time, Pallas kernels for 7%

profile of v2, /device:TPU:131, one launch (start us, length us, event | category | flops | bytes accessed | tf_op | source)
XLA Modules:
  0.0 58.7 jit_solution(1632536547829429832)
XLA Ops:
  0.0 1.4 %shard_map.64 = (bf16[1,4,1152]{2,1,0:T(4,128)(2,1)S(1)}, bf16[24,4,1152]{2,1,0:T(4,128)(2,1)}) custom-call(s32[4]{0:T(128)} %ids_ref.1, bf16[4,1024]{1,0:T(4,128)(2,1)} %blocks_ref.1), custom_call_target="tpu_custom_call" | custom-call | tf_op jit(solution)/shard_map/pallas_call | solution.py:168
  1.4 17.4 %all-to-all-start = ((bf16[24,4,1152]{2,1,0:T(4,128)(2,1)}), bf16[24,4,1152]{2,1,0:T(4,128)(2,1)S(1)}, u32[]{:S(2)}, u32[]{:S(2)}) async-start(bf16[24,4,1152]{2,1,0:T(4,128)(2,1)} %get-tuple-element.12), calls=%async_computation | async-start | bytes 442368 | tf_op jit(solution)/shard_map/all_to_all | solution.py:190
  18.8 2.2 %collective-permute-start = (bf16[1,4,1152]{2,1,0:T(4,128)(2,1)S(1)}, bf16[1,4,1152]{2,1,0:T(4,128)(2,1)S(1)}, u32[]{:S(2)}, u32[]{:S(2)}) collective-permute-start(bf16[1,4,1152]{2,1,0:T(4,128)(2,1)S(1)} %get-tuple-element.13), channel_id=1, source_target_pairs={{384,0},{480,96},{576,192},{672,288},{0,384},{96,480},{192,576},{2... | collective-permute-start | bytes 27656 | tf_op jit(solution)/shard_map/ppermute | solution.py:194
  21.0 3.4 %collective-permute-done = bf16[1,4,1152]{2,1,0:T(4,128)(2,1)S(1)} collective-permute-done((bf16[1,4,1152]{2,1,0:T(4,128)(2,1)S(1)}, bf16[1,4,1152]{2,1,0:T(4,128)(2,1)S(1)}, u32[]{:S(2)}, u32[]{:S(2)}) %collective-permute-start) | collective-permute-done | bytes 9248 | tf_op jit(solution)/shard_map/ppermute | solution.py:194
  24.3 10.4 %all-to-all-done = bf16[24,4,1152]{2,1,0:T(4,128)(2,1)S(1)} async-done(((bf16[24,4,1152]{2,1,0:T(4,128)(2,1)}), bf16[24,4,1152]{2,1,0:T(4,128)(2,1)S(1)}, u32[]{:S(2)}, u32[]{:S(2)}) %all-to-all-start) | async-done | bytes 221216 | tf_op jit(solution)/shard_map/all_to_all | solution.py:190
  34.7 0.1 reshape.16
  34.8 0.0 copy-start
  34.8 0.0 copy-start.1
  34.8 0.0 copy-start.2
  34.8 1.0 %broadcast_in_dim.2 = bf16[4,96,1152]{2,1,0:T(8,128)(2,1)} broadcast(bf16[96,1152]{1,0:T(8,128)(2,1)S(1)} %reshape.16), dimensions={1,2} | broadcast | bytes 1105920 | tf_op jit(solution)/shard_map/broadcast_in_dim | solution.py:180
  35.8 4.3 %all-to-all-start.1 = ((bf16[4,96,1152]{2,1,0:T(8,128)(2,1)}), bf16[4,96,1152]{2,1,0:T(8,128)(2,1)S(1)}, u32[]{:S(2)}, u32[]{:S(2)}) async-start(bf16[4,96,1152]{2,1,0:T(8,128)(2,1)} %broadcast_in_dim.2), calls=%async_computation.1 | async-start | bytes 1769472 | tf_op jit(solution)/shard_map/all_to_all | solution.py:181
  40.1 4.4 %collective-permute-start.1 = (bf16[2,4,1152]{2,1,0:T(4,128)(2,1)S(1)}, bf16[2,4,1152]{2,1,0:T(4,128)(2,1)S(1)}, u32[]{:S(2)}, u32[]{:S(2)}) collective-permute-start(bf16[2,4,1152]{2,1,0:T(4,128)(2,1)S(1)} %pad_maximum_fusion), channel_id=1, source_target_pairs={{192,0},{288,96},{0,192},{96,288},{576,384},{672,480},{384,576},{4... | collective-permute-start | bytes 55304 | tf_op jit(solution)/shard_map/ppermute | solution.py:194
  44.5 1.4 %collective-permute-done.1 = bf16[2,4,1152]{2,1,0:T(4,128)(2,1)S(1)} collective-permute-done((bf16[2,4,1152]{2,1,0:T(4,128)(2,1)S(1)}, bf16[2,4,1152]{2,1,0:T(4,128)(2,1)S(1)}, u32[]{:S(2)}, u32[]{:S(2)}) %collective-permute-start.1) | collective-permute-done | bytes 18464 | tf_op jit(solution)/shard_map/ppermute | solution.py:194
  45.9 4.0 %collective-permute-start.2 = (bf16[4,4,1152]{2,1,0:T(4,128)(2,1)S(1)}, bf16[4,4,1152]{2,1,0:T(4,128)(2,1)S(1)}, u32[]{:S(2)}, u32[]{:S(2)}) collective-permute-start(bf16[4,4,1152]{2,1,0:T(4,128)(2,1)S(1)} %constant_dynamic-update-slice_fusion), channel_id=1, source_target_pairs={{96,0},{0,96},{288,192},{192,288},{480,384},{384,480},{672,576},{5... | collective-permute-start | bytes 110600 | tf_op jit(solution)/shard_map/ppermute | solution.py:198
  50.6 0.2 collective-permute-done.2
  50.8 0.0 copy-done
  50.8 0.0 copy-done.1
  50.8 0.0 copy-done.2
  50.8 4.3 %shard_map.65 = (f32[1024,128]{1,0:T(8,128)S(1)}, s32[1,128]{1,0:T(1,128)S(1)}, bf16[128,384]{1,0:T(8,128)(2,1)S(1)}) custom-call(s32[1,1]{1,0:T(1,128)} %bitcast.1.me_ref, bf16[128,4096]{1,0:T(8,128)(2,1)S(1)} %copy-done, bf16[16,1152]{1,0:T(8,128)(2,1)S(1)} %reshape.19.held_ref, bf16[16,1152]{1,0:T(8,128)(2,1)S(1)} %reshape.20.rest_ref, ...), custom_call_target="tpu_custom_call" | custom-call | tf_op jit(solution)/shard_map/pallas_call | solution.py:121
  55.1 0.0 all-to-all-done.1
  55.1 3.6 %shard_map.66 = bf16[3072,256]{1,0:T(8,128)(2,1)} custom-call(s32[1,1]{1,0:T(1,128)S(6)} %copy.8.count_ref, bf16[384,1152]{1,0:T(8,128)(2,1)S(1)} %bitcast.2, bf16[128,384]{1,0:T(8,128)(2,1)S(1)} %get-tuple-element.16.pick_ref, f32[1024,128]{1,0:T(8,128)S(1)} %get-tuple-element.17.z_ref, s32[1,128]{1,0:T(1,128)S(1)} %get-tuple-element.18.coarse_ref, ...), custom_call_target="tpu_custom_call" | custom-call | tf_op jit(solution)/shard_map/pallas_call | solution.py:139
  (5 shorter events, 0.1 us)
Async XLA Ops:
  1.4 33.3 %all-to-all-start = ((bf16[24,4,1152]{2,1,0:T(4,128)(2,1)}), bf16[24,4,1152]{2,1,0:T(4,128)(2,1)S(1)}, u32[]{:S(2)}, u32[]{:S(2)}) async-start(bf16[24,4,1152]{2,1,0:T(4,128)(2,1)} %get-tuple-element.12), calls=%async_computation | async-start | bytes 442368 | tf_op jit(solution)/shard_map/all_to_all | solution.py:190
  18.8 5.5 %collective-permute-start = (bf16[1,4,1152]{2,1,0:T(4,128)(2,1)S(1)}, bf16[1,4,1152]{2,1,0:T(4,128)(2,1)S(1)}, u32[]{:S(2)}, u32[]{:S(2)}) collective-permute-start(bf16[1,4,1152]{2,1,0:T(4,128)(2,1)S(1)} %get-tuple-element.13), channel_id=1, source_target_pairs={{384,0},{480,96},{576,192},{672,288},{0,384},{96,480},{192,576},{2... | collective-permute-start | bytes 27656 | tf_op jit(solution)/shard_map/ppermute | solution.py:194
  34.8 16.0 %copy-start = (bf16[128,4096]{1,0:T(8,128)(2,1)S(1)}, bf16[128,4096]{1,0:T(8,128)(2,1)}, u32[]{:S(2)}) copy-start(bf16[128,4096]{1,0:T(8,128)(2,1)} %a_ref.1) | copy-start | bytes 3145732
  34.8 16.0 %copy-start.1 = (s32[1,128]{1,0:T(1,128)S(1)}, s32[1,128]{1,0:T(1,128)}, u32[]{:S(2)}) copy-start(s32[1,128]{1,0:T(1,128)} %row_ref.3) | copy-start | bytes 1540
  34.8 16.0 %copy-start.2 = (s32[1,128]{1,0:T(1,128)S(1)}, s32[1,128]{1,0:T(1,128)}, u32[]{:S(2)}) copy-start(s32[1,128]{1,0:T(1,128)} %col_ref.1) | copy-start | bytes 1540
  35.8 19.3 %all-to-all-start.1 = ((bf16[4,96,1152]{2,1,0:T(8,128)(2,1)}), bf16[4,96,1152]{2,1,0:T(8,128)(2,1)S(1)}, u32[]{:S(2)}, u32[]{:S(2)}) async-start(bf16[4,96,1152]{2,1,0:T(8,128)(2,1)} %broadcast_in_dim.2), calls=%async_computation.1 | async-start | bytes 1769472 | tf_op jit(solution)/shard_map/all_to_all | solution.py:181
  40.1 5.8 %collective-permute-start.1 = (bf16[2,4,1152]{2,1,0:T(4,128)(2,1)S(1)}, bf16[2,4,1152]{2,1,0:T(4,128)(2,1)S(1)}, u32[]{:S(2)}, u32[]{:S(2)}) collective-permute-start(bf16[2,4,1152]{2,1,0:T(4,128)(2,1)S(1)} %pad_maximum_fusion), channel_id=1, source_target_pairs={{192,0},{288,96},{0,192},{96,288},{576,384},{672,480},{384,576},{4... | collective-permute-start | bytes 55304 | tf_op jit(solution)/shard_map/ppermute | solution.py:194
  45.9 4.8 %collective-permute-start.2 = (bf16[4,4,1152]{2,1,0:T(4,128)(2,1)S(1)}, bf16[4,4,1152]{2,1,0:T(4,128)(2,1)S(1)}, u32[]{:S(2)}, u32[]{:S(2)}) collective-permute-start(bf16[4,4,1152]{2,1,0:T(4,128)(2,1)S(1)} %constant_dynamic-update-slice_fusion), channel_id=1, source_target_pairs={{96,0},{0,96},{288,192},{192,288},{480,384},{384,480},{672,576},{5... | collective-permute-start | bytes 110600 | tf_op jit(solution)/shard_map/ppermute | solution.py:198
